TPU v7x, 512 devices: a whole 4x8x8 slice. The times are simulated.
512 devices in a mesh: role: 4 (over x), cls: 128 (over y, z, core).
Axes of the slice: x: 4, y: 8, z: 8, core: 2. Of those that a mesh axis runs over, the one named last changes fastest.
Arguments:
- features: bfloat16 [1024, 512], P('cls', 'role'), may hold values from -160 to 160, as said below
- centres: bfloat16 [1572864, 512], P(('role', 'cls')), may hold values from -0.25 to 0.25
- samples: int32 [512, 1024], P(('role', 'cls')), may hold values from 0 to 3071, as said below
- counts: int32 [512], P(('role', 'cls')), may hold values from 64 to 1024, as said below
- label_row: int32 [1024], replicated, may hold values from 0 to 3071, as said below
- owner: int32 [1024], replicated, may hold values from 0 to 511, as said below
Outputs:
- feature_grad: float32 [1024, 512], P('cls', 'role')
- centre_grad: bfloat16 [512, 1024, 512], P(('role', 'cls'))
- loss: float32 [1024], P('cls')
Inputs may be any that keep to these rules, and one draw needn't show every extreme that they name: `features`: scaled values with spread per image and per feature. `samples`: entries of one shard are distinct; only the first counts[q] entries of shard q are used. `counts`: each count is 1024 divided by 1, 2, 4, 8 or 16; some shard has exactly 1024. label_row[i] stands among the first counts[owner[i]] entries of samples[owner[i]]. `owner`: index of the owning shard along role+cls; shards with more used slots own more images.
All inputs are finite; a program needn't handle non-finite values.
Results may differ from a plain program's by a relative error of at most 0.0061.
Values may be sent and summed in bfloat16 or wider, within the bound.
A program may use at most 64 MiB of HBM per device.

v0:
```python
import math
import jax
import jax.numpy as jnp
from jax import lax
from jax.sharding import PartitionSpec as P

logit_scale = 64.0
margin_cos = math.cos(0.5)
margin_sin = math.sin(0.5)
epsilon = 1e-05


def body(features, centres, samples, counts, label_row, owner):
    cls_size = lax.axis_size("cls")
    img_rows = features.shape[0]
    images = img_rows * cls_size
    values = features.astype(jnp.float32)
    col_mean = lax.psum(jnp.sum(values, 0), "cls") / images
    centred = values - col_mean
    col_var = lax.psum(jnp.sum(centred * centred, 0), "cls") / images
    inv_std = lax.rsqrt(col_var + epsilon)
    normed = centred * inv_std
    norm_sq = lax.psum(jnp.sum(normed * normed, 1), "role")
    inv_norm = lax.rsqrt(norm_sq + epsilon)
    unit_feats = normed * inv_norm[:, None]
    widened = lax.all_gather(unit_feats.astype(jnp.bfloat16), "role", axis=1, tiled=True)
    gathered = lax.all_gather(widened, "cls", axis=0, tiled=True)
    shard_id = lax.axis_index("role") * cls_size + lax.axis_index("cls")
    row_ids = samples[0]
    live_count = counts[0]
    picked = jnp.take(centres, row_ids, axis=0).astype(jnp.float32)
    w_inv = lax.rsqrt(jnp.sum(picked * picked, 1) + epsilon)
    w_unit = picked * w_inv[:, None]
    w_round = w_unit.astype(jnp.bfloat16)
    cosine = lax.dot_general(
        gathered, w_round, (((1,), (1,)), ((), ())), preferred_element_type=jnp.float32
    )
    slot_ids = jnp.arange(row_ids.shape[0], dtype=jnp.int32)
    usable = slot_ids < live_count
    positive = (
        (owner[:, None] == shard_id) & (label_row[:, None] == row_ids[None, :]) & usable[None, :]
    )
    sine_part = jnp.sqrt(jnp.maximum(1.0 - cosine * cosine, 0.0))
    target = cosine * margin_cos - sine_part * margin_sin
    logits = logit_scale * jnp.where(positive, target, cosine)
    exp_terms = jnp.where(usable[None, :], jnp.exp(logits), jnp.float32(0.0))
    part_sum = jnp.sum(exp_terms, 1)
    part_pos = jnp.sum(jnp.where(positive, logits, jnp.float32(0.0)), 1)
    partition_sum, positive_logit = lax.psum((part_sum, part_pos), ("role", "cls"))
    loss_all = jnp.log(partition_sum) - positive_logit
    loss = lax.dynamic_slice_in_dim(loss_all, lax.axis_index("cls") * img_rows, img_rows, 0)
    grad_logit = logit_scale * (exp_terms / partition_sum[:, None] - positive.astype(jnp.float32))
    grad_round = grad_logit.astype(jnp.bfloat16)
    back_rows = lax.dot_general(
        grad_round, gathered, (((0,), (0,)), ((), ())), preferred_element_type=jnp.float32
    )
    radial_rows = jnp.sum(w_unit * back_rows, 1, keepdims=True)
    centre_grad = ((back_rows - w_unit * radial_rows) * w_inv[:, None]).astype(jnp.bfloat16)[None]
    full_grad = jnp.dot(grad_round, w_round, preferred_element_type=jnp.float32)
    split_grad = lax.psum_scatter(full_grad, "role", scatter_dimension=1, tiled=True)
    grad_unit = lax.psum_scatter(split_grad, "cls", scatter_dimension=0, tiled=True)
    radial_part = lax.psum(jnp.sum(unit_feats * grad_unit, 1), "role")
    grad_normed = (grad_unit - unit_feats * radial_part[:, None]) * inv_norm[:, None]
    grad_total, cross_total = lax.psum(
        (jnp.sum(grad_normed, 0), jnp.sum(grad_normed * normed, 0)), "cls"
    )
    feature_grad = (grad_normed - grad_total / images - normed * (cross_total / images)) * inv_std
    return (feature_grad, centre_grad, loss)


def solution(mesh):
    return jax.shard_map(
        body,
        mesh=mesh,
        in_specs=(
            P("cls", "role"),
            P(("role", "cls"), None),
            P(("role", "cls"), None),
            P(("role", "cls")),
            P(),
            P(),
        ),
        out_specs=(P("cls", "role"), P(("role", "cls"), None, None), P("cls")),
        check_vma=False,
    )
```

profile of v0, /device:TPU:1, one launch (start us, length us, event | category | flops | bytes accessed | tf_op | source)
XLA Modules:
  0.0 1212.5 jit_solution(9806286267377754459)
XLA Ops:
  7.2 0.8 convert_reduce_fusion
  8.1 254.6 %psum.56 = f32[128]{0:T(128)S(1)} all-reduce(f32[128]{0:T(128)S(1)} %convert_reduce_fusion), channel_id=1, replica_groups=mesh['role'=4,'cls'=128] {'cls'}, use_global_device_ids=true, to_apply=%region_1.0 | all-reduce | flops 128 | bytes 1024 | tf_op jit(solution)/shard_map/psum | solution.py:18
  262.7 0.7 fusion.31
  263.4 251.2 %psum.57 = f32[128]{0:T(128)S(1)} all-reduce(f32[128]{0:T(128)S(1)} %fusion.31), channel_id=1, replica_groups=mesh['role'=4,'cls'=128] {'cls'}, use_global_device_ids=true, to_apply=%region_3.0 | all-reduce | flops 128 | bytes 1024 | tf_op jit(solution)/shard_map/psum | solution.py:20
  514.6 0.8 fusion.27
  515.4 8.5 psum.58
  523.9 0.8 fusion.23
  524.6 8.4 all_gather.6
  533.1 0.0 reduce-scatter.2.cloned.1.call-start
  533.1 0.7 compare_select_fusion
  533.9 5.1 gather_fusion
  539.0 2.3 copy.13
  542.0 1.5 fusion.8
  543.5 66.5 %all-gather.2.cloned.1.call-done = bf16[1024,512]{1,0:T(8,128)(2,1)} async-done(((bf16[8,512]{1,0:T(8,128)(2,1)}), bf16[1024,512]{1,0:T(8,128)(2,1)}) %all-gather.2.cloned.1.call-update) | async-done | bytes 1048592 | tf_op jit(solution)/shard_map/all_gather | solution.py:27
  610.0 7.4 select_reduce_fusion
  617.4 96.5 %all-reduce.1 = (f32[1024]{0:T(1024)S(1)}, f32[1024]{0:T(1024)S(1)}) all-reduce(f32[1024]{0:T(1024)S(1)} %get-tuple-element.13, f32[1024]{0:T(1024)S(1)} %get-tuple-element.12), channel_id=1, replica_groups=mesh['role'=4,'cls'=128] {'role','cls'}, use_global_device_ids=true, to_apply=%region_8.9 | all-reduce | flops 2048 | bytes 16384 | tf_op jit(solution)/shard_map/psum | solution.py:49
  713.9 3.5 multiply_convert_fusion
  717.4 1.3 copy-done.2
  718.8 2.6 fusion.10
  721.4 0.0 all-reduce.5.cloned.1.call-start
  721.4 1.3 dynamic-slice
  723.4 4.8 fusion.4
  728.2 22.0 %reduce-scatter.2.cloned.1.call-done = f32[1024,128]{1,0:T(8,128)} async-done(((f32[1024,512]{1,0:T(8,128)}), f32[1024,128]{1,0:T(8,128)}) %reduce-scatter.2.cloned.1.call-update) | async-done | bytes 524304 | tf_op jit(solution)/shard_map/reduce_scatter | solution.py:60
  750.2 3.3 fusion.9
  753.5 2.3 copy.14
  755.8 188.5 %all-reduce.5.cloned.1.call-done = f32[1024,128]{1,0:T(8,128)} async-done(((f32[1024,128]{1,0:T(8,128)}), f32[1024,128]{1,0:T(8,128)}) %all-reduce.5.cloned.1.call-update) | async-done | bytes 524304
  944.3 0.9 fusion.24
  945.2 0.6 dynamic_slice.3
  945.8 8.4 psum.60
  954.1 0.8 fusion.34
  954.9 249.7 %all-reduce.2 = (f32[128]{0:T(128)S(1)}, f32[128]{0:T(128)S(1)}) all-reduce(f32[128]{0:T(128)S(1)} %get-tuple-element.15, f32[128]{0:T(128)S(1)} %get-tuple-element.14), channel_id=1, replica_groups=mesh['role'=4,'cls'=128] {'cls'}, use_global_device_ids=true, to_apply=%region_16.17 | all-reduce | flops 256 | bytes 2048 | tf_op jit(solution)/shard_map/psum | solution.py:64
  1204.6 1.4 fusion.30
  (27 shorter events, 0.2 us)
Async XLA Ops:
  7.2 526.7 %copy-start = (bf16[3072,512]{1,0:T(8,128)(2,1)S(1)}, bf16[3072,512]{1,0:T(8,128)(2,1)}, u32[]{:S(2)}) copy-start(bf16[3072,512]{1,0:T(8,128)(2,1)} %param.7) | copy-start | bytes 9437188
  7.2 602.8 %all-gather.2.cloned.1.call-start = ((), (), s32[]{:S(2)}) async-start(), calls=%async_computation.1 | async-start | bytes 1056768 | tf_op jit(solution)/shard_map/all_gather | solution.py:27
  533.1 217.1 %reduce-scatter.2.cloned.1.call-start = ((), (), s32[]{:S(2)}) async-start(), calls=%async_computation.2 | async-start | bytes 2621440 | tf_op jit(solution)/shard_map/reduce_scatter | solution.py:60
  533.8 8.1 copy-start.4
  533.9 8.1 copy-start.6
  539.0 71.0 %copy-start.5 = (s32[1024]{0:T(1024)S(1)}, s32[1024]{0:T(1024)}, u32[]{:S(2)}) copy-start(s32[1024]{0:T(1024)} %param.10) | copy-start | bytes 12292
  713.9 4.9 copy-start.1
  717.4 1.3 copy-start.2
  721.4 222.9 %all-reduce.5.cloned.1.call-start = ((), (), s32[]{:S(2)}) async-start(), calls=%async_computation.3 | async-start | bytes 1048576
  750.2 194.1 %copy-start.3 = (bf16[8,128]{1,0:T(8,128)(2,1)S(1)}, bf16[8,128]{1,0:T(8,128)(2,1)}, u32[]{:S(2)}) copy-start(bf16[8,128]{1,0:T(8,128)(2,1)} %param.6) | copy-start | bytes 6148
Sparse Core Ops, SparseCore 0:
  533.2 76.7 all-gather.1
  721.5 28.6 reduce-scatter.1
  753.7 190.5 all-reduce.4
where the time goes:
time: 1210 us
  blocking collectives  877 us (72%)
  waiting for transfers between devices  277 us (23%)
  other arithmetic  15.3 us (1%)
  between operations  15.2 us (1%)
  matrix products  14.8 us (1%)
  local copies, waits for them, and re-layouts  12.9 us (1%)
    psum x1, blocking collectives, body(): col_mean = lax.psum(jnp.sum(values, 0), 'cls') / images  255 us
    psum x1, blocking collectives, body(): col_var = lax.psum(jnp.sum(centred * centred, 0), 'cls') / images  251 us
    psum x1, blocking collectives, body(): lax.psum((jnp.sum(grad_normed, 0), jnp.sum(grad_normed * normed, 0)), 'cls')  250 us
    unnamed x4, waiting for transfers between devices  189 us
    psum x1, blocking collectives, body(): lax.psum((part_sum, part_pos), ('role', 'cls'))  96.5 us
    all_gather x1, waiting for transfers between devices, body(): gathered = lax.all_gather(widened, 'cls', axis=0, tiled=True)  66.5 us
  transfers between devices with their start and end apart: 3, of which 3 were waited for; matrix products, arithmetic and copies ran while one was open for 2% of the time, Pallas kernels for 0%

commit v1 on v0

--- a/solution.py
+++ b/solution.py
@@ -46,7 +46,7 @@
     exp_terms = jnp.where(usable[None, :], jnp.exp(logits), jnp.float32(0.0))
     part_sum = jnp.sum(exp_terms, 1)
     part_pos = jnp.sum(jnp.where(positive, logits, jnp.float32(0.0)), 1)
-    partition_sum, positive_logit = lax.psum((part_sum, part_pos), ("role", "cls"))
+    partition_sum, positive_logit = lax.psum(lax.psum((part_sum, part_pos), "cls"), "role")
     loss_all = jnp.log(partition_sum) - positive_logit
     loss = lax.dynamic_slice_in_dim(loss_all, lax.axis_index("cls") * img_rows, img_rows, 0)
     grad_logit = logit_scale * (exp_terms / partition_sum[:, None] - positive.astype(jnp.float32))

time: 1210 us -> 1390 us (1.15)
  blocking collectives: 877 us -> 1050 us
    psum x1 -> x3, blocking collectives: 96.5 us -> 261 us  [the longest x1 246 us: body(): lax.psum((part_sum, part_pos), 'cls')]
  transfers between devices with their start and end apart: 3 -> 3, of which waited for: 3 -> 3; matrix products, arithmetic and copies ran while one was open for 2% -> 1% of each run, Pallas kernels for 0% -> 0%
where the time goes in v1:
time: 1390 us
  blocking collectives  1050 us (76%)
  waiting for transfers between devices  282 us (20%)
  other arithmetic  15.3 us (1%)
  between operations  15.2 us (1%)
  matrix products  14.8 us (1%)
    psum x1, blocking collectives, body(): col_mean = lax.psum(jnp.sum(values, 0), 'cls') / images  255 us
    psum x1, blocking collectives, body(): lax.psum((jnp.sum(grad_normed, 0), jnp.sum(grad_normed * normed, 0)), 'cls')  254 us
    psum x1, blocking collectives, body(): col_var = lax.psum(jnp.sum(centred * centred, 0), 'cls') / images  251 us
    psum x1, blocking collectives, body(): lax.psum((part_sum, part_pos), 'cls')  246 us
    unnamed x4, waiting for transfers between devices  191 us
    all_gather x1, waiting for transfers between devices, body(): gathered = lax.all_gather(widened, 'cls', axis=0, tiled=True)  66.5 us
  transfers between devices with their start and end apart: 3, of which 3 were waited for; matrix products, arithmetic and copies ran while one was open for 1% of the time, Pallas kernels for 0%

profile of v1, /device:TPU:1, one launch (start us, length us, event | category | flops | bytes accessed | tf_op | source)
XLA Modules:
  0.0 1386.0 jit_solution(1073263015068995166)
XLA Ops:
  7.2 0.8 convert_reduce_fusion
  8.1 254.6 %psum.70 = f32[128]{0:T(128)S(1)} all-reduce(f32[128]{0:T(128)S(1)} %convert_reduce_fusion), channel_id=1, replica_groups=mesh['role'=4,'cls'=128] {'cls'}, use_global_device_ids=true, to_apply=%region_1.0 | all-reduce | flops 128 | bytes 1024 | tf_op jit(solution)/shard_map/psum | solution.py:18
  262.7 0.7 fusion.31
  263.4 251.2 %psum.71 = f32[128]{0:T(128)S(1)} all-reduce(f32[128]{0:T(128)S(1)} %fusion.31), channel_id=1, replica_groups=mesh['role'=4,'cls'=128] {'cls'}, use_global_device_ids=true, to_apply=%region_3.0 | all-reduce | flops 128 | bytes 1024 | tf_op jit(solution)/shard_map/psum | solution.py:20
  514.6 0.8 fusion.27
  515.4 8.5 psum.72
  523.9 0.8 fusion.23
  524.6 8.4 all_gather.6
  533.1 0.7 compare_select_fusion
  533.9 5.1 gather_fusion
  539.0 2.3 copy.13
  542.0 1.5 fusion.8
  543.5 66.5 %all-gather.2.cloned.1.call-done = bf16[1024,512]{1,0:T(8,128)(2,1)} async-done(((bf16[8,512]{1,0:T(8,128)(2,1)}), bf16[1024,512]{1,0:T(8,128)(2,1)}) %all-gather.2.cloned.1.call-update) | async-done | bytes 1048592 | tf_op jit(solution)/shard_map/all_gather | solution.py:27
  610.0 7.4 select_reduce_fusion
  617.4 246.4 %psum.73 = f32[1024]{0:T(1024)S(1)} all-reduce(f32[1024]{0:T(1024)S(1)} %get-tuple-element.13), channel_id=1, replica_groups=mesh['role'=4,'cls'=128] {'cls'}, use_global_device_ids=true, to_apply=%region_8.9 | all-reduce | flops 1024 | bytes 8192 | tf_op jit(solution)/shard_map/psum | solution.py:49
  863.8 8.4 psum.74
  872.2 3.5 multiply_convert_fusion
  875.8 1.3 copy-done.2
  877.1 2.6 fusion.10
  879.7 1.3 dynamic-slice
  881.7 4.8 fusion.4
  886.5 24.7 %reduce-scatter.2.cloned.1.call-done = f32[1024,128]{1,0:T(8,128)} async-done(((f32[1024,512]{1,0:T(8,128)}), f32[1024,128]{1,0:T(8,128)}) %reduce-scatter.2.cloned.1.call-update) | async-done | bytes 524304 | tf_op jit(solution)/shard_map/reduce_scatter | solution.py:60
  911.2 3.3 fusion.9
  914.5 190.9 %all-reduce.4.cloned.1.call-done = f32[1024,128]{1,0:T(8,128)} async-done(((f32[1024,128]{1,0:T(8,128)}), f32[1024,128]{1,0:T(8,128)}) %all-reduce.4.cloned.1.call-update) | async-done | bytes 524304
  1105.4 0.9 fusion.24
  1106.3 2.3 copy.14
  1108.6 8.4 psum.75
  1117.0 0.8 fusion.34
  1117.7 253.7 %all-reduce.1 = (f32[128]{0:T(128)S(1)}, f32[128]{0:T(128)S(1)}, f32[1024]{0:T(1024)S(1)}) all-reduce(f32[128]{0:T(128)S(1)} %get-tuple-element.15, f32[128]{0:T(128)S(1)} %get-tuple-element.14, f32[1024]{0:T(1024)S(1)} %get-tuple-element.12), channel_id=1, replica_groups=mesh['role'=4,'cls'=128] {'cls'}, use_global_device_ids=true, to_apply=%region_17.18 | all-reduce | flops 1280 | bytes 10240 | tf_op jit(solution)/shard_map/psum | solution.py:64
  1371.5 6.0 psum.79
  1377.5 0.6 dynamic_slice.3
  1378.1 1.4 fusion.30
  (29 shorter events, 0.3 us)
Async XLA Ops:
  7.2 526.7 %copy-start = (bf16[3072,512]{1,0:T(8,128)(2,1)S(1)}, bf16[3072,512]{1,0:T(8,128)(2,1)}, u32[]{:S(2)}) copy-start(bf16[3072,512]{1,0:T(8,128)(2,1)} %param.7) | copy-start | bytes 9437188
  7.2 602.8 %all-gather.2.cloned.1.call-start = ((), (), s32[]{:S(2)}) async-start(), calls=%async_computation.1 | async-start | bytes 1056768 | tf_op jit(solution)/shard_map/all_gather | solution.py:27
  533.1 378.1 %reduce-scatter.2.cloned.1.call-start = ((), (), s32[]{:S(2)}) async-start(), calls=%async_computation.2 | async-start | bytes 2621440 | tf_op jit(solution)/shard_map/reduce_scatter | solution.py:60
  533.8 8.1 copy-start.4
  533.9 8.1 copy-start.6
  539.0 71.0 %copy-start.5 = (s32[1024]{0:T(1024)S(1)}, s32[1024]{0:T(1024)}, u32[]{:S(2)}) copy-start(s32[1024]{0:T(1024)} %param.10) | copy-start | bytes 12292
  872.2 4.9 copy-start.1
  875.7 1.3 copy-start.2
  879.7 225.7 %all-reduce.4.cloned.1.call-start = ((), (), s32[]{:S(2)}) async-start(), calls=%async_computation.3 | async-start | bytes 1048576
  886.5 218.9 %copy-start.3 = (bf16[8,128]{1,0:T(8,128)(2,1)S(1)}, bf16[8,128]{1,0:T(8,128)(2,1)}, u32[]{:S(2)}) copy-start(bf16[8,128]{1,0:T(8,128)(2,1)} %param.6) | copy-start | bytes 6148
Sparse Core Ops, SparseCore 0:
  533.2 76.7 all-gather.1
  879.8 31.3 reduce-scatter.1
  914.8 190.6 all-reduce.3

commit v2 on v0

--- a/solution.py
+++ b/solution.py
@@ -15,7 +15,7 @@
     img_rows = features.shape[0]
     images = img_rows * cls_size
     values = features.astype(jnp.float32)
-    col_mean = lax.psum(jnp.sum(values, 0), "cls") / images
+    col_mean = jnp.sum(lax.all_gather(jnp.sum(values, 0), "cls"), axis=0) / images
     centred = values - col_mean
     col_var = lax.psum(jnp.sum(centred * centred, 0), "cls") / images
     inv_std = lax.rsqrt(col_var + epsilon)

time: 1210 us -> 1010 us (0.83)
  blocking collectives: 877 us -> 670 us
    psum x1 -> x0, blocking collectives: 255 us -> none  [body(): col_mean = lax.psum(jnp.sum(values, 0), 'cls') / images]
    all_gather x0 -> x1, blocking collectives: none -> 52 us  [body(): lax.all_gather(jnp.sum(values, 0), 'cls')]
where the time goes in v2:
time: 1010 us
  blocking collectives  670 us (66%)
  waiting for transfers between devices  281 us (28%)
  other arithmetic  15.4 us (2%)
  between operations  15.2 us (2%)
  matrix products  14.8 us (1%)
  local copies, waits for them, and re-layouts  12.9 us (1%)
    psum x1, blocking collectives, body(): lax.psum((jnp.sum(grad_normed, 0), jnp.sum(grad_normed * normed, 0)), 'cls')  250 us
    psum x1, blocking collectives, body(): col_var = lax.psum(jnp.sum(centred * centred, 0), 'cls') / images  246 us
    unnamed x4, waiting for transfers between devices  189 us
    psum x1, blocking collectives, body(): lax.psum((part_sum, part_pos), ('role', 'cls'))  96.5 us
    all_gather x1, waiting for transfers between devices, body(): gathered = lax.all_gather(widened, 'cls', axis=0, tiled=True)  69.9 us
    all_gather x1, blocking collectives, body(): lax.all_gather(jnp.sum(values, 0), 'cls')  52 us
    reduce_scatter x1, waiting for transfers between devices, body(): lax.psum_scatter(full_grad, 'role', scatter_dimension=1, tiled=True)  22 us
  transfers between devices with their start and end apart: 3, of which 3 were waited for; matrix products, arithmetic and copies ran while one was open for 2% of the time, Pallas kernels for 0%

profile of v2, /device:TPU:1, one launch (start us, length us, event | category | flops | bytes accessed | tf_op | source)
XLA Modules:
  0.0 1008.7 jit_solution(10704165766303852030)
XLA Ops:
  7.2 0.8 convert_reduce_fusion
  8.1 52.0 %all-gather.1 = f32[128,1,128]{2,1,0:T(1,128)S(1)} all-gather(f32[1,1,128]{2,1,0:T(1,128)S(1)} %bitcast.18), channel_id=2, replica_groups=mesh['role'=4,'cls'=128] {'cls'}, dimensions={0}, use_global_device_ids=true | all-gather | bytes 66048 | tf_op jit(solution)/shard_map/all_gather | solution.py:18
  60.0 0.2 reduce_sum.100
  60.2 0.7 fusion.31
  60.9 246.3 %psum.49 = f32[128]{0:T(128)S(1)} all-reduce(f32[128]{0:T(128)S(1)} %fusion.31), channel_id=1, replica_groups=mesh['role'=4,'cls'=128] {'cls'}, use_global_device_ids=true, to_apply=%region_3.0 | all-reduce | flops 128 | bytes 1024 | tf_op jit(solution)/shard_map/psum | solution.py:20
  307.2 0.8 fusion.27
  308.0 8.5 psum.50
  316.5 0.8 fusion.23
  317.3 8.4 all_gather.14
  325.7 0.0 reduce-scatter.2.cloned.1.call-start
  325.7 0.7 compare_select_fusion
  326.5 5.1 gather_fusion
  331.6 2.3 copy.13
  334.6 1.5 fusion.8
  336.1 69.9 %all-gather.4.cloned.1.call-done = bf16[1024,512]{1,0:T(8,128)(2,1)} async-done(((bf16[8,512]{1,0:T(8,128)(2,1)}), bf16[1024,512]{1,0:T(8,128)(2,1)}) %all-gather.4.cloned.1.call-update) | async-done | bytes 1048592 | tf_op jit(solution)/shard_map/all_gather | solution.py:27
  406.0 7.4 select_reduce_fusion
  413.4 96.5 %all-reduce.1 = (f32[1024]{0:T(1024)S(1)}, f32[1024]{0:T(1024)S(1)}) all-reduce(f32[1024]{0:T(1024)S(1)} %get-tuple-element.13, f32[1024]{0:T(1024)S(1)} %get-tuple-element.12), channel_id=1, replica_groups=mesh['role'=4,'cls'=128] {'role','cls'}, use_global_device_ids=true, to_apply=%region_8.9 | all-reduce | flops 2048 | bytes 16384 | tf_op jit(solution)/shard_map/psum | solution.py:49
  509.9 3.5 multiply_convert_fusion
  513.5 1.3 copy-done.2
  514.8 2.6 fusion.10
  517.5 1.3 dynamic-slice
  519.4 4.8 fusion.4
  524.2 22.0 %reduce-scatter.2.cloned.1.call-done = f32[1024,128]{1,0:T(8,128)} async-done(((f32[1024,512]{1,0:T(8,128)}), f32[1024,128]{1,0:T(8,128)}) %reduce-scatter.2.cloned.1.call-update) | async-done | bytes 524304 | tf_op jit(solution)/shard_map/reduce_scatter | solution.py:60
  546.2 3.3 fusion.9
  549.6 2.3 copy.14
  551.8 188.7 %all-reduce.5.cloned.1.call-done = f32[1024,128]{1,0:T(8,128)} async-done(((f32[1024,128]{1,0:T(8,128)}), f32[1024,128]{1,0:T(8,128)}) %all-reduce.5.cloned.1.call-update) | async-done | bytes 524304
  740.5 0.9 fusion.24
  741.4 0.6 dynamic_slice.3
  742.0 8.4 psum.52
  750.4 0.8 fusion.34
  751.1 249.7 %all-reduce.2 = (f32[128]{0:T(128)S(1)}, f32[128]{0:T(128)S(1)}) all-reduce(f32[128]{0:T(128)S(1)} %get-tuple-element.15, f32[128]{0:T(128)S(1)} %get-tuple-element.14), channel_id=1, replica_groups=mesh['role'=4,'cls'=128] {'cls'}, use_global_device_ids=true, to_apply=%region_16.17 | all-reduce | flops 256 | bytes 2048 | tf_op jit(solution)/shard_map/psum | solution.py:64
  1000.8 1.4 fusion.30
  (28 shorter events, 0.2 us)
Async XLA Ops:
  7.2 319.3 %copy-start = (bf16[3072,512]{1,0:T(8,128)(2,1)S(1)}, bf16[3072,512]{1,0:T(8,128)(2,1)}, u32[]{:S(2)}) copy-start(bf16[3072,512]{1,0:T(8,128)(2,1)} %param.7) | copy-start | bytes 9437188
  7.2 398.8 %all-gather.4.cloned.1.call-start = ((), (), s32[]{:S(2)}) async-start(), calls=%async_computation.1 | async-start | bytes 1056768 | tf_op jit(solution)/shard_map/all_gather | solution.py:27
  325.7 220.5 %reduce-scatter.2.cloned.1.call-start = ((), (), s32[]{:S(2)}) async-start(), calls=%async_computation.2 | async-start | bytes 2621440 | tf_op jit(solution)/shard_map/reduce_scatter | solution.py:60
  326.5 8.1 copy-start.4
  326.5 8.1 copy-start.6
  331.6 74.4 %copy-start.5 = (s32[1024]{0:T(1024)S(1)}, s32[1024]{0:T(1024)}, u32[]{:S(2)}) copy-start(s32[1024]{0:T(1024)} %param.10) | copy-start | bytes 12292
  509.9 4.9 copy-start.1
  513.5 1.3 copy-start.2
  517.4 223.1 %all-reduce.5.cloned.1.call-start = ((), (), s32[]{:S(2)}) async-start(), calls=%async_computation.3 | async-start | bytes 1048576
  546.2 194.3 %copy-start.3 = (bf16[8,128]{1,0:T(8,128)(2,1)S(1)}, bf16[8,128]{1,0:T(8,128)(2,1)}, u32[]{:S(2)}) copy-start(bf16[8,128]{1,0:T(8,128)(2,1)} %param.6) | copy-start | bytes 6148
Sparse Core Ops, SparseCore 0:
  325.8 80.1 all-gather.3
  517.5 28.6 reduce-scatter.1
  549.8 190.7 all-reduce.4
